TPU v7x, 512 devices: a whole 4x8x8 slice. The times are simulated.
512 devices in a mesh: dp: 32 (over x, z), table: 16 (over y, core).
Axes of the slice: x: 4, y: 8, z: 8, core: 2. Of those that a mesh axis runs over, the one named last changes fastest.
Arguments:
- dense_feats: bfloat16 [65536, 13], P(('dp', 'table')), may hold values from -6 to 6
- lookup_ids: int32 [32, 8, 65536], P('table', None, 'dp'), may hold values from 0 to 2047
- lookup_counts: int32 [32, 65536], P('table', 'dp'), may hold values from 0 to 8
- shard_table: int32 [32], replicated, may hold values from 0 to 25, as said below
- embed_tables: bfloat16 [32, 2048, 128], P('table'), may hold values from -6 to 6
- first_layer: bfloat16 [13, 512], replicated, may hold values from -1.75 to 1.75
- first_offset: float32 [512], replicated, may hold values from -3 to 3
- second_layer: bfloat16 [512, 256], replicated, may hold values from -0.25 to 0.25
- second_offset: float32 [256], replicated, may hold values from -3 to 3
- third_layer: bfloat16 [256, 128], replicated, may hold values from -0.375 to 0.375
- third_offset: float32 [128], replicated, may hold values from -3 to 3
- cross_down: bfloat16 [3456, 512], P(None, 'table'), may hold values from -0.109375 to 0.109375
- cross_up: bfloat16 [512, 3456], P('table'), may hold values from -0.25 to 0.25
- cross_bias: float32 [3456], replicated, may hold values from -3 to 3
- cotangent: bfloat16 [65536, 3456], P(('dp', 'table')), may hold values from -0.059814453 to 0.059814453
Outputs:
- table_grad: float32 [32, 2048, 128], P('table', 'dp')
- first_layer_grad: float32 [13, 512], replicated
- first_offset_grad: float32 [512], replicated
- second_layer_grad: float32 [512, 256], replicated
- second_offset_grad: float32 [256], replicated
- third_layer_grad: float32 [256, 128], replicated
- third_offset_grad: float32 [128], replicated
- cross_bias_grad: float32 [3456], replicated
Inputs may be any that keep to these rules, and one draw needn't show every extreme that they name: `shard_table`: every table has at least one shard.
All inputs are finite; a program needn't handle non-finite values.
Results may differ from a plain program's by a relative error of at most 0.0085.
Values may be sent and summed in bfloat16 or wider, within the bound.
No kernel may reach another device: no remote copies, remote signals or barrier semaphores. Data moves between devices by JAX's collectives and lax.ppermute only.
A program may use at most 64 MiB of HBM per device.

v0:
```python
import math
import jax
import jax.numpy as jnp
from jax import lax
from jax.sharding import PartitionSpec as P

TABLES = 26


def silu_slope(value):
    sigmoid = 1.0 / (1.0 + jnp.exp(-value))
    return sigmoid * (1.0 + value * (1.0 - sigmoid))


def hit_counts(index_block, count_block, row_total):
    iota_rows = lax.broadcasted_iota(jnp.int32, (index_block.shape[1], row_total), 1)
    totals = jnp.zeros((index_block.shape[1], row_total), jnp.bfloat16)
    for slot_index in range(index_block.shape[0]):
        matched = (index_block[slot_index][:, None] == iota_rows) & (
            count_block[:, None] > slot_index
        )
        totals = totals + matched.astype(jnp.bfloat16)
    return totals


def split_blocks(shard_index, shard_count, block_size):
    hot_total, batch_total = shard_index.shape
    blocks = batch_total // block_size
    index_blocks = shard_index.reshape(hot_total, blocks, block_size).transpose(1, 0, 2)
    count_blocks = shard_count.reshape(blocks, block_size)
    return (index_blocks, count_blocks, blocks)


def pool_shard(table_rows, shard_index, shard_count, block_size):
    index_blocks, count_blocks, blocks = split_blocks(shard_index, shard_count, block_size)

    def pool_one_block(inputs):
        hit_table = hit_counts(inputs[0], inputs[1], table_rows.shape[0])
        return jnp.dot(hit_table, table_rows, preferred_element_type=jnp.float32)

    pooled = lax.map(pool_one_block, (index_blocks, count_blocks))
    return pooled.reshape(shard_index.shape[1], table_rows.shape[1])


def shard_gradient(shard_index, shard_count, grad_rows, row_total, block_size):
    index_blocks, count_blocks, blocks = split_blocks(shard_index, shard_count, block_size)
    grad_blocks = grad_rows.reshape(blocks, block_size, grad_rows.shape[1])

    def shard_one_block(running, inputs):
        hit_table = hit_counts(inputs[0], inputs[1], row_total)
        update = lax.dot_general(
            hit_table, inputs[2], (((0,), (0,)), ((), ())), preferred_element_type=jnp.float32
        )
        return (running + update, None)

    result, unused = lax.scan(
        shard_one_block,
        jnp.zeros((row_total, grad_rows.shape[1]), jnp.float32),
        (index_blocks, count_blocks, grad_blocks),
    )
    return result


def bottom_pass(
    dense_rows, first_layer, first_offset, second_layer, second_offset, third_layer, third_offset
):
    first_pre = jnp.dot(dense_rows, first_layer, preferred_element_type=jnp.float32) + first_offset
    first_act = jax.nn.silu(first_pre).astype(jnp.bfloat16)
    second_pre = (
        jnp.dot(first_act, second_layer, preferred_element_type=jnp.float32) + second_offset
    )
    second_act = jax.nn.silu(second_pre).astype(jnp.bfloat16)
    third_pre = jnp.dot(second_act, third_layer, preferred_element_type=jnp.float32) + third_offset
    bottom_out = jax.nn.silu(third_pre).astype(jnp.bfloat16)
    return (bottom_out, (first_pre, first_act, second_pre, second_act, third_pre))


def bottom_back(dense_rows, saved, second_layer, third_layer, bottom_grad):
    first_pre, first_act, second_pre, second_act, third_pre = saved
    contract = (((0,), (0,)), ((), ()))
    back_dims = (((1,), (1,)), ((), ()))
    third_delta = (silu_slope(third_pre) * bottom_grad.astype(jnp.float32)).astype(jnp.bfloat16)
    third_grad = lax.dot_general(
        second_act, third_delta, contract, preferred_element_type=jnp.float32
    )
    third_bias = jnp.sum(third_delta.astype(jnp.float32), axis=0)
    second_back = lax.dot_general(
        third_delta, third_layer, back_dims, preferred_element_type=jnp.float32
    )
    second_delta = (silu_slope(second_pre) * second_back).astype(jnp.bfloat16)
    second_grad = lax.dot_general(
        first_act, second_delta, contract, preferred_element_type=jnp.float32
    )
    second_bias = jnp.sum(second_delta.astype(jnp.float32), axis=0)
    first_back = lax.dot_general(
        second_delta, second_layer, back_dims, preferred_element_type=jnp.float32
    )
    first_delta = (silu_slope(first_pre) * first_back).astype(jnp.bfloat16)
    first_grad = lax.dot_general(
        dense_rows, first_delta, contract, preferred_element_type=jnp.float32
    )
    first_bias = jnp.sum(first_delta.astype(jnp.float32), axis=0)
    return (first_grad, first_bias, second_grad, second_bias, third_grad, third_bias)


def local(
    dense_feats,
    lookup_ids,
    lookup_counts,
    shard_table,
    embed_tables,
    first_layer,
    first_offset,
    second_layer,
    second_offset,
    third_layer,
    third_offset,
    cross_down,
    cross_up,
    cross_bias,
    cotangent,
):
    local_shards, row_total, width = embed_tables.shape
    batch_group = lookup_ids.shape[2]
    block_size = math.gcd(batch_group, 1024)
    examples = dense_feats.shape[0]
    back_dims = (((1,), (1,)), ((), ()))
    pooled = jnp.stack(
        [
            pool_shard(
                embed_tables[shard_pos], lookup_ids[shard_pos], lookup_counts[shard_pos], block_size
            )
            for shard_pos in range(local_shards)
        ],
        axis=1,
    ).astype(jnp.bfloat16)
    arrived = lax.all_to_all(pooled, "table", split_axis=0, concat_axis=1, tiled=True)
    table_onehot = (
        shard_table[:, None] == lax.broadcasted_iota(jnp.int32, (shard_table.shape[0], TABLES), 1)
    ).astype(jnp.bfloat16)
    table_pooled = jnp.einsum(
        "bse,st->bte", arrived, table_onehot, preferred_element_type=jnp.float32
    ).astype(jnp.bfloat16)
    bottom_out, saved = bottom_pass(
        dense_feats,
        first_layer,
        first_offset,
        second_layer,
        second_offset,
        third_layer,
        third_offset,
    )
    cross_input = jnp.concatenate([bottom_out[:, None, :], table_pooled], axis=1).reshape(
        examples, -1
    )
    down_whole = lax.all_gather(cross_down, "table", axis=1, tiled=True)
    up_whole = lax.all_gather(cross_up, "table", axis=0, tiled=True)
    low_rank = jnp.dot(cross_input, down_whole, preferred_element_type=jnp.float32).astype(
        jnp.bfloat16
    )
    mixing = jnp.dot(low_rank, up_whole, preferred_element_type=jnp.float32) + cross_bias
    cot_float = cotangent.astype(jnp.float32)
    mix_grad = cot_float * cross_input.astype(jnp.float32)
    bias_part = jnp.sum(mix_grad, axis=0)
    rank_grad = lax.dot_general(
        mix_grad.astype(jnp.bfloat16), up_whole, back_dims, preferred_element_type=jnp.float32
    ).astype(jnp.bfloat16)
    input_grad = (
        cot_float * (mixing + 1.0)
        + lax.dot_general(rank_grad, down_whole, back_dims, preferred_element_type=jnp.float32)
    ).astype(jnp.bfloat16)
    input_grad = input_grad.reshape(examples, TABLES + 1, width)
    bottom_grad = input_grad[:, 0, :]
    shard_grads = jnp.einsum(
        "bte,st->bse", input_grad[:, 1:, :], table_onehot, preferred_element_type=jnp.float32
    ).astype(jnp.bfloat16)
    returned = lax.all_to_all(shard_grads, "table", split_axis=1, concat_axis=0, tiled=True)
    local_grad = jnp.stack(
        [
            shard_gradient(
                lookup_ids[shard_pos],
                lookup_counts[shard_pos],
                returned[:, shard_pos, :],
                row_total,
                block_size,
            )
            for shard_pos in range(local_shards)
        ],
        axis=0,
    )
    table_grad = lax.psum_scatter(local_grad, "dp", scatter_dimension=1, tiled=True)
    partial_grads = bottom_back(dense_feats, saved, second_layer, third_layer, bottom_grad)
    summed = lax.psum(
        (
            partial_grads[0],
            partial_grads[1],
            partial_grads[2],
            partial_grads[3],
            partial_grads[4],
            partial_grads[5],
            bias_part,
        ),
        ("dp", "table"),
    )
    return (table_grad, summed[0], summed[1], summed[2], summed[3], summed[4], summed[5], summed[6])


def solution(mesh):
    placed = (
        P(("dp", "table"), None),
        P("table", None, "dp"),
        P("table", "dp"),
        P(),
        P("table", None, None),
        P(),
        P(),
        P(),
        P(),
        P(),
        P(),
        P(None, "table"),
        P("table", None),
        P(),
        P(("dp", "table"), None),
    )
    return jax.shard_map(
        local,
        mesh=mesh,
        in_specs=placed,
        out_specs=(P("table", "dp", None), P(), P(), P(), P(), P(), P(), P()),
        check_vma=False,
    )
```

profile of v0, /device:TPU:8, one launch (start us, length us, event | category | flops | bytes accessed | tf_op | source)
XLA Modules:
  0.0 667.9 jit_solution(7342675556975713716)
XLA Ops:
  7.2 0.7 all-gather.3.cloned.1.call-update
  8.0 0.7 all-gather.5.cloned.1.call-update
  8.7 0.9 fusion.208
  9.6 0.8 slice_reduce_fusion.1
  10.4 1.3 slice_bitcast_fusion.1
  11.8 33.8 %while.42 = (s32[]{:T(128)}, bf16[2,1024,128]{2,1,0:T(8,128)(2,1)S(1)}, s32[2,8,1024]{2,1,0:T(8,128)S(1)}, s32[2,1024]{1,0:T(2,128)S(1)}, bf16[2048,128]{1,0:T(8...) while((s32[]{:T(128)}, ...), condition=%wide.region_1.2_spmd, body=%wide.region_0.1_spmd.sunk | while | flops 620765184 | bytes 1167617 | solution.py:41
  11.9 16.7 %fusion.244 = bf16[2,1024,128]{2,1,0:T(8,128)(2,1)S(1)} fusion(bf16[2,1024,128]{2,1,0:T(8,128)(2,1)S(1)} %get-tuple-element.590, s32[]{:T(128)} %get-tuple-element.589, bf16[2048,128]{1,0:T(8,128)(2,1)S(1)} %get-tuple-element.607, s32[1024]{0:T(1024)S(1)} %bitcast.227, s32[1024]{0:T(1024)S(1)} %bitcast.221, s32[1024]{0:T(1024)S(1)} %bitcast.222, ...), kind=kOutput, calls=%fused_computation.41.clone.1 | convolution fusion | flops 620756992 | bytes 1089540 | tf_op jit(solution)/shard_map/while/body/eval_jaxpr/dot_general | solution.py:39
  28.8 16.7 %fusion.244 = bf16[2,1024,128]{2,1,0:T(8,128)(2,1)S(1)} fusion(bf16[2,1024,128]{2,1,0:T(8,128)(2,1)S(1)} %get-tuple-element.590, s32[]{:T(128)} %get-tuple-element.589, bf16[2048,128]{1,0:T(8,128)(2,1)S(1)} %get-tuple-element.607, s32[1024]{0:T(1024)S(1)} %bitcast.227, s32[1024]{0:T(1024)S(1)} %bitcast.221, s32[1024]{0:T(1024)S(1)} %bitcast.222, ...), kind=kOutput, calls=%fused_computation.41.clone.1 | convolution fusion | flops 620756992 | bytes 1089540 | tf_op jit(solution)/shard_map/while/body/eval_jaxpr/dot_general | solution.py:39
  45.7 33.8 %while.43 = (s32[]{:T(128)}, bf16[2,1024,128]{2,1,0:T(8,128)(2,1)S(1)}, s32[2,8,1024]{2,1,0:T(8,128)S(1)}, s32[2,1024]{1,0:T(2,128)S(1)}, bf16[2048,128]{1,0:T(8...) while((s32[]{:T(128)}, ...), condition=%wide.region_3.4_spmd, body=%wide.region_2.3_spmd.sunk | while | flops 620765184 | bytes 1167617 | solution.py:41
  45.8 16.7 %fusion.247 = bf16[2,1024,128]{2,1,0:T(8,128)(2,1)S(1)} fusion(bf16[2,1024,128]{2,1,0:T(8,128)(2,1)S(1)} %get-tuple-element.548, s32[]{:T(128)} %get-tuple-element.547, bf16[2048,128]{1,0:T(8,128)(2,1)S(1)} %get-tuple-element.565, s32[1024]{0:T(1024)S(1)} %bitcast.235, s32[1024]{0:T(1024)S(1)} %bitcast.229, s32[1024]{0:T(1024)S(1)} %bitcast.230, ...), kind=kOutput, calls=%fused_computation.100.clone.1 | convolution fusion | flops 620756992 | bytes 1089540 | tf_op jit(solution)/shard_map/while/body/eval_jaxpr/dot_general | solution.py:39
  62.7 16.7 %fusion.247 = bf16[2,1024,128]{2,1,0:T(8,128)(2,1)S(1)} fusion(bf16[2,1024,128]{2,1,0:T(8,128)(2,1)S(1)} %get-tuple-element.548, s32[]{:T(128)} %get-tuple-element.547, bf16[2048,128]{1,0:T(8,128)(2,1)S(1)} %get-tuple-element.565, s32[1024]{0:T(1024)S(1)} %bitcast.235, s32[1024]{0:T(1024)S(1)} %bitcast.229, s32[1024]{0:T(1024)S(1)} %bitcast.230, ...), kind=kOutput, calls=%fused_computation.100.clone.1 | convolution fusion | flops 620756992 | bytes 1089540 | tf_op jit(solution)/shard_map/while/body/eval_jaxpr/dot_general | solution.py:39
  79.6 9.5 %copy.44 = bf16[2048,2,128]{2,1,0:T(2,128)(2,1)} copy(bf16[2048,2,128]{2,0,1:T(8,128)(2,1)S(1)} %pad_maximum_fusion.1) | data formatting | bytes 2097152 | tf_op jit(solution)/shard_map/stack | solution.py:128
  89.1 9.8 %all-to-all-start = ((bf16[2048,2,128]{2,1,0:T(2,128)(2,1)}), bf16[2048,2,128]{2,1,0:T(2,128)(2,1)S(1)}, u32[]{:S(2)}, u32[]{:S(2)}) async-start(bf16[2048,2,128]{2,1,0:T(2,128)(2,1)} %copy.44), calls=%async_computation | async-start | bytes 2097152 | tf_op jit(solution)/shard_map/all_to_all | solution.py:137
  99.0 0.2 convolution_add_fusion.2
  99.5 0.2 convolution_add_fusion.4
  99.9 24.2 %all-to-all-done = bf16[2048,2,128]{2,1,0:T(2,128)(2,1)S(1)} async-done(((bf16[2048,2,128]{2,1,0:T(2,128)(2,1)}), bf16[2048,2,128]{2,1,0:T(2,128)(2,1)S(1)}, u32[]{:S(2)}, u32[]{:S(2)}) %all-to-all-start) | async-done | bytes 1048608 | tf_op jit(solution)/shard_map/all_to_all | solution.py:137
  124.2 1.1 copy.46
  125.3 0.5 fusion.191
  125.9 0.5 pad_maximum_fusion.2
  126.4 1.3 copy.49
  127.7 1.0 copy.50
  128.8 6.5 fusion.187
  135.3 5.4 fusion.188
  140.7 1.0 copy.51
  141.8 1.0 slice.188
  142.7 1.9 copy.52
  144.7 0.5 fusion.192
  145.2 1.4 copy.53
  146.6 6.3 all-to-all-start.1
  153.0 0.6 convert_reduce_fusion.2
  153.6 0.8 convert_reduce_fusion.1
  154.4 0.9 fusion.204
  155.3 1.1 fusion.205
  156.4 21.2 %all-to-all-done.1 = bf16[128,32,128]{2,0,1:T(8,128)(2,1)S(1)} async-done(((bf16[128,32,128]{2,0,1:T(8,128)(2,1)}), bf16[128,32,128]{2,0,1:T(8,128)(2,1)S(1)}, u32[]{:S(2)}, u32[]{:S(2)}) %all-to-all-start.1) | async-done | bytes 1048608 | tf_op jit(solution)/shard_map/all_to_all | solution.py:177
  177.9 30.7 %while.44 = (s32[]{:T(128)}, f32[2048,128]{1,0:T(8,128)}, s32[2,8,1024]{2,1,0:T(8,128)S(1)}, s32[2,1024]{1,0:T(2,128)S(1)}, bf16[2,1024,128]{2,1,0:T(8,128)(2,1)...) while((s32[]{:T(128)}, f32[2048,128]{1,0:T(8,128)}, ...), condition=%wide.region_5.6_spmd.clone, body=%wide.region_4.5_spmd.clone.sunk | while | flops 621289472 | bytes 2478347 | solution.py:56
  178.2 14.5 %fusion.250 = f32[2048,128]{1,0:T(8,128)} fusion(s32[1024]{0:T(1024)S(1)} %bitcast.211, s32[1024]{0:T(1024)S(1)} %bitcast.205, s32[1024]{0:T(1024)S(1)} %bitcast.206, s32[1024]{0:T(1024)S(1)} %bitcast.207, s32[1024]{0:T(1024)S(1)} %bitcast.208, s32[1024]{0:T(1024)S(1)} %bitcast.209, s32[1024]{0:T(1024)S(1)} %bitcast.210, s32[1024]{0:T(1024)S(1)} %bitcast.204, ...), kind=kOutput, calls=%fused_computation.166.clone.1 | convolution fusion | flops 621281280 | bytes 2400261 | tf_op jit(solution)/shard_map/while/body/eval_jaxpr/dot_general | solution.py:51
  192.9 15.7 %fusion.250 = f32[2048,128]{1,0:T(8,128)} fusion(s32[1024]{0:T(1024)S(1)} %bitcast.211, s32[1024]{0:T(1024)S(1)} %bitcast.205, s32[1024]{0:T(1024)S(1)} %bitcast.206, s32[1024]{0:T(1024)S(1)} %bitcast.207, s32[1024]{0:T(1024)S(1)} %bitcast.208, s32[1024]{0:T(1024)S(1)} %bitcast.209, s32[1024]{0:T(1024)S(1)} %bitcast.210, s32[1024]{0:T(1024)S(1)} %bitcast.204, ...), kind=kOutput, calls=%fused_computation.166.clone.1 | convolution fusion | flops 621281280 | bytes 2400261 | tf_op jit(solution)/shard_map/while/body/eval_jaxpr/dot_general | solution.py:51
  208.6 27.9 %while.45 = (s32[]{:T(128)}, f32[2048,128]{1,0:T(8,128)S(1)}, s32[2,8,1024]{2,1,0:T(8,128)S(1)}, s32[2,1024]{1,0:T(2,128)S(1)}, bf16[2,1024,128]{2,1,0:T(8,128)(...) while((s32[]{:T(128)}, f32[2048,128]{1,0:T(8,128)S(1)}, ...), condition=%wide.region_7.8_spmd.clone, body=%wide.region_6.7_spmd.clone.sunk | while | flops 621289472 | bytes 2478347 | solution.py:56
  209.0 13.7 %fusion.253 = f32[2048,128]{1,0:T(8,128)S(1)} fusion(s32[1024]{0:T(1024)S(1)} %bitcast.219, s32[1024]{0:T(1024)S(1)} %bitcast.213, s32[1024]{0:T(1024)S(1)} %bitcast.214, s32[1024]{0:T(1024)S(1)} %bitcast.215, s32[1024]{0:T(1024)S(1)} %bitcast.216, s32[1024]{0:T(1024)S(1)} %bitcast.217, s32[1024]{0:T(1024)S(1)} %bitcast.218, ...), kind=kOutput, calls=%fused_computation.235.clone.1 | convolution fusion | flops 621281280 | bytes 2400261 | tf_op jit(solution)/shard_map/while/body/eval_jaxpr/dot_general | solution.py:51
  222.8 13.7 %fusion.253 = f32[2048,128]{1,0:T(8,128)S(1)} fusion(s32[1024]{0:T(1024)S(1)} %bitcast.219, s32[1024]{0:T(1024)S(1)} %bitcast.213, s32[1024]{0:T(1024)S(1)} %bitcast.214, s32[1024]{0:T(1024)S(1)} %bitcast.215, s32[1024]{0:T(1024)S(1)} %bitcast.216, s32[1024]{0:T(1024)S(1)} %bitcast.217, s32[1024]{0:T(1024)S(1)} %bitcast.218, ...), kind=kOutput, calls=%fused_computation.235.clone.1 | convolution fusion | flops 621281280 | bytes 2400261 | tf_op jit(solution)/shard_map/while/body/eval_jaxpr/dot_general | solution.py:51
  236.5 2.9 pad_maximum_fusion
  239.5 0.3 fusion.189
  239.7 0.2 convert_reduce_fusion
  240.2 104.6 %all-reduce = (f32[13,512]{1,0:T(8,128)}, f32[512]{0:T(512)}, f32[256]{0:T(256)}, f32[128]{0:T(128)}, f32[3456]{0:T(1024)}) all-reduce(f32[13,512]{1,0:T(8,128)S(1)} %convolution_bitcast_fusion, f32[512]{0:T(512)S(1)} %get-tuple-element.277, f32[256]{0:T(256)S(1)} %copy-done.15, ...), channel_id=1, replica_groups=mesh['dp'=32,'table'=16] {'dp','table'}, use_global_device_ids=true, to_apply=%region_9.10 | all-reduce | flops 11008 | bytes 88064 | tf_op jit(solution)/shard_map/psum | solution.py:193
  344.8 87.7 %all-reduce.4.cloned.1.call-done = (f32[512,256]{1,0:T(8,128)}, f32[256,128]{1,0:T(8,128)}) async-done(((f32[512,256]{1,0:T(8,128)}, f32[256,128]{1,0:T(8,128)}), (f32[512,256]{1,0:T(8,128)}, f32[256,128]{1,0:T(8,128)})) %all-reduce.4.cloned.1.call-update) | async-done | bytes 655376 | tf_op jit(solution)/shard_map/psum | solution.py:193
  432.5 225.0 %reduce-scatter.2.cloned.1.call-done = f32[2,64,128]{2,1,0:T(8,128)} async-done(((f32[2,2048,128]{2,1,0:T(8,128)}), f32[2,64,128]{2,1,0:T(8,128)}) %reduce-scatter.2.cloned.1.call-update) | async-done | bytes 65552 | tf_op jit(solution)/shard_map/reduce_scatter | solution.py:191
  657.5 1.9 copy.85
  659.4 1.6 copy.86
  (86 shorter events, 2.7 us)
Async XLA Ops:
  7.2 92.0 %copy-start = (bf16[512,256]{1,0:T(8,128)(2,1)S(1)}, bf16[512,256]{1,0:T(8,128)(2,1)}, u32[]{:S(2)}) copy-start(bf16[512,256]{1,0:T(8,128)(2,1)} %param.30) | copy-start | bytes 786436
  7.2 121.6 %all-gather.3.cloned.1.call-start = ((), (), s32[]{:S(2)}) async-start(), calls=%async_computation.3 | async-start | bytes 3760128 | tf_op jit(solution)/shard_map/all_gather | solution.py:156
  7.9 120.9 %all-gather.5.cloned.1.call-start = ((), (), s32[]{:S(2)}) async-start(), calls=%async_computation.4 | async-start | bytes 3760128 | tf_op jit(solution)/shard_map/all_gather | solution.py:157
  79.5 19.5 %copy-start.8 = (bf16[13,512]{1,0:T(8,128)(2,1)S(1)}, bf16[13,512]{1,0:T(8,128)(2,1)}, u32[]{:S(2)}) copy-start(bf16[13,512]{1,0:T(8,128)(2,1)} %param.28) | copy-start | bytes 39940
  79.5 19.5 %copy-start.9 = (bf16[128,13]{0,1:T(8,128)(2,1)S(1)}, bf16[128,13]{0,1:T(8,128)(2,1)}, u32[]{:S(2)}) copy-start(bf16[128,13]{0,1:T(8,128)(2,1)} %param.23) | copy-start | bytes 9988
  79.5 19.5 %copy-start.11 = (f32[512]{0:T(512)S(1)}, f32[512]{0:T(512)}, u32[]{:S(2)}) copy-start(f32[512]{0:T(512)} %param.29) | copy-start | bytes 6148
  79.5 19.7 %copy-start.18 = (f32[256]{0:T(256)S(1)}, f32[256]{0:T(256)}, u32[]{:S(2)}) copy-start(f32[256]{0:T(256)} %param.31) | copy-start | bytes 3076
  79.5 19.9 %copy-start.16 = (bf16[256,128]{1,0:T(8,128)(2,1)S(1)}, bf16[256,128]{1,0:T(8,128)(2,1)}, u32[]{:S(2)}) copy-start(bf16[256,128]{1,0:T(8,128)(2,1)} %param.32) | copy-start | bytes 196612
  79.5 19.9 %copy-start.19 = (f32[128]{0:T(128)S(1)}, f32[128]{0:T(128)}, u32[]{:S(2)}) copy-start(f32[128]{0:T(128)} %param.33) | copy-start | bytes 1540
  89.1 34.9 %all-to-all-start = ((bf16[2048,2,128]{2,1,0:T(2,128)(2,1)}), bf16[2048,2,128]{2,1,0:T(2,128)(2,1)S(1)}, u32[]{:S(2)}, u32[]{:S(2)}) async-start(bf16[2048,2,128]{2,1,0:T(2,128)(2,1)} %copy.44), calls=%async_computation | async-start | bytes 2097152 | tf_op jit(solution)/shard_map/all_to_all | solution.py:137
  99.0 26.3 %copy-start.12 = (s32[32]{0:T(128)S(1)}, s32[32]{0:T(128)}, u32[]{:S(2)}) copy-start(s32[32]{0:T(128)} %param.26) | copy-start | bytes 388
  99.2 56.1 %copy-start.6 = (f32[128,512]{1,0:T(8,128)}, f32[128,512]{1,0:T(8,128)S(1)}, u32[]{:S(2)}) copy-start(f32[128,512]{1,0:T(8,128)S(1)} %convolution_add_fusion.2) | copy-start | bytes 786436
  99.5 26.4 %copy-start.20 = (f32[128,256]{1,0:T(8,128)}, f32[128,256]{1,0:T(8,128)S(1)}, u32[]{:S(2)}) copy-start(f32[128,256]{1,0:T(8,128)S(1)} %convolution_add_fusion.3) | copy-start | bytes 393220
  125.3 3.5 copy-start.3
  128.7 6.6 copy-start.1
  140.7 3.9 copy-start.13
  144.7 9.0 %copy-start.17 = (bf16[256,128]{1,0:T(8,128)(2,1)S(1)}, bf16[256,128]{1,0:T(8,128)(2,1)}, u32[]{:S(2)}) copy-start(bf16[256,128]{1,0:T(8,128)(2,1)} %param.32) | copy-start | bytes 196612
  144.7 9.0 %copy-start.21 = (f32[128,256]{1,0:T(8,128)S(1)}, f32[128,256]{1,0:T(8,128)}, u32[]{:S(2)}) copy-start(f32[128,256]{1,0:T(8,128)} %copy-done.20) | copy-start | bytes 393220
  146.6 31.0 %all-to-all-start.1 = ((bf16[128,32,128]{2,0,1:T(8,128)(2,1)}), bf16[128,32,128]{2,0,1:T(8,128)(2,1)S(1)}, u32[]{:S(2)}, u32[]{:S(2)}) async-start(bf16[128,32,128]{2,0,1:T(8,128)(2,1)} %copy.53), calls=%async_computation.1 | async-start | bytes 2097152 | tf_op jit(solution)/shard_map/all_to_all | solution.py:177
  152.9 279.6 %all-reduce.4.cloned.1.call-start = ((), (), s32[]{:S(2)}) async-start(), calls=%async_computation.6 | async-start | bytes 1310720 | tf_op jit(solution)/shard_map/psum | solution.py:193
  154.4 23.5 %copy-start.22 = (bf16[128,256]{1,0:T(8,128)(2,1)}, bf16[128,256]{1,0:T(8,128)(2,1)S(1)}, u32[]{:S(2)}) copy-start(bf16[128,256]{1,0:T(8,128)(2,1)S(1)} %get-tuple-element.280) | copy-start | bytes 196612
  156.4 501.1 %reduce-scatter.2.cloned.1.call-start = ((), (), s32[]{:S(2)}) async-start(), calls=%async_computation.5 | async-start | bytes 2162688 | tf_op jit(solution)/shard_map/reduce_scatter | solution.py:191
  177.9 30.7 %copy-start.5 = (f32[2048,128]{1,0:T(8,128)S(1)}, f32[2048,128]{1,0:T(8,128)}, u32[]{:S(2)}) copy-start(f32[2048,128]{1,0:T(8,128)} %custom-call.1) | copy-start | bytes 3145732
  236.5 2.9 copy-start.2
  236.5 2.9 copy-start.4
  236.5 3.2 copy-start.7
  236.5 3.2 copy-start.23
  239.4 0.7 copy-start.10
  239.4 0.8 copy-start.14
  239.4 0.8 copy-start.15
Sparse Core Ops, SparseCore 0:
  10.1 48.4 all-gather.2
  60.7 47.3 all-gather.4
  159.3 273.1 all-reduce.3
  437.9 219.5 reduce-scatter.1
where the time goes:
time: 674 us; the launch traced here: 668 us
  waiting for transfers between devices  360 us (53%)
  matrix products  141 us (21%)
  blocking collectives  105 us (16%)
  local copies, waits for them, and re-layouts  25.8 us (4%)
  starting transfers between devices  16.3 us (2%)
  between operations  14.7 us (2%)
    reduce_scatter x1, waiting for transfers between devices, local(): lax.psum_scatter(local_grad, 'dp', scatter_dimension=1, tiled=True)  225 us
    psum x1, blocking collectives, local(): lax.psum((partial_grads[0], partial_grads[1], partial_grads[2], partial_g...  105 us
    psum x1, waiting for transfers between devices, local(): lax.psum((partial_grads[0], partial_grads[1], partial_grads[2], partial_g...  87.7 us
    dot_general x4, matrix products, pool_one_block(): return jnp.dot(hit_table, table_rows, preferred_element_type=jnp.float32)  66.9 us
    dot_general x4, matrix products, shard_one_block(): lax.dot_general(hit_table, inputs[2], (((0,), (0,)), ((), ())), preferred...  57.6 us
    all_to_all x1, waiting for transfers between devices, local(): lax.all_to_all(pooled, 'table', split_axis=0, concat_axis=1, tiled=True)  24.2 us
    all_to_all x1, waiting for transfers between devices, local(): lax.all_to_all(shard_grads, 'table', split_axis=1, concat_axis=0, tiled=T...  21.2 us
  transfers between devices with their start and end apart: 6, of which 4 were waited for; matrix products, arithmetic and copies ran while one was open for 23% of the time, Pallas kernels for 0%

commit v1 on v0

--- a/solution.py
+++ b/solution.py
@@ -190,18 +190,17 @@
     )
     table_grad = lax.psum_scatter(local_grad, "dp", scatter_dimension=1, tiled=True)
     partial_grads = bottom_back(dense_feats, saved, second_layer, third_layer, bottom_grad)
-    summed = lax.psum(
-        (
-            partial_grads[0],
-            partial_grads[1],
-            partial_grads[2],
-            partial_grads[3],
-            partial_grads[4],
-            partial_grads[5],
-            bias_part,
-        ),
-        ("dp", "table"),
-    )
+    in_array = (
+        partial_grads[0],
+        partial_grads[1],
+        partial_grads[2],
+        partial_grads[3],
+        partial_grads[4],
+        partial_grads[5],
+        bias_part,
+    )
+    u_next = lax.psum(in_array, "table")
+    summed = lax.psum(u_next, "dp")
     return (table_grad, summed[0], summed[1], summed[2], summed[3], summed[4], summed[5], summed[6])
 
 

time: 674 us -> 683 us (1.013)
  blocking collectives: 105 us -> 191 us
  waiting for transfers between devices: 360 us -> 282 us
    reduce_scatter x1, waiting for transfers between devices: 225 us -> 136 us  [local(): lax.psum_scatter(local_grad, 'dp', scatter_dimension=1, tiled=True)]
    psum x1 -> x2, blocking collectives: 105 us -> 191 us  [the longest x1 144 us: local(): summed = lax.psum(u_next, 'dp')]
    psum x1 -> x2, waiting for transfers between devices: 87.7 us -> 120 us  [the longest x1 120 us: local(): u_next = lax.psum(in_array, 'table')]
    all_to_all x1, waiting for transfers between devices: 21.2 us -> 0.01 us  [local(): lax.all_to_all(shard_grads, 'table', split_axis=1, concat_axis=0, tiled=T...]
  transfers between devices with their start and end apart: 6 -> 7, of which waited for: 4 -> 3; matrix products, arithmetic and copies ran while one was open for 23% -> 22% of each run, Pallas kernels for 0% -> 0%
where the time goes in v1:
time: 683 us; the launch traced here: 677 us
  waiting for transfers between devices  282 us (41%)
  blocking collectives  191 us (28%)
  matrix products  141 us (21%)
  local copies, waits for them, and re-layouts  25.8 us (4%)
  starting transfers between devices  16.3 us (2%)
  between operations  14.7 us (2%)
    psum x1, blocking collectives, local(): summed = lax.psum(u_next, 'dp')  144 us
    reduce_scatter x1, waiting for transfers between devices, local(): lax.psum_scatter(local_grad, 'dp', scatter_dimension=1, tiled=True)  136 us
    psum x1, waiting for transfers between devices, local(): u_next = lax.psum(in_array, 'table')  120 us
    dot_general x4, matrix products, pool_one_block(): return jnp.dot(hit_table, table_rows, preferred_element_type=jnp.float32)  66.9 us
    dot_general x4, matrix products, shard_one_block(): lax.dot_general(hit_table, inputs[2], (((0,), (0,)), ((), ())), preferred...  57.5 us
    psum x1, blocking collectives, local(): u_next = lax.psum(in_array, 'table')  47.9 us
    all_to_all x1, waiting for transfers between devices, local(): lax.all_to_all(pooled, 'table', split_axis=0, concat_axis=1, tiled=True)  24.2 us
  transfers between devices with their start and end apart: 7, of which 3 were waited for; matrix products, arithmetic and copies ran while one was open for 22% of the time, Pallas kernels for 0%

profile of v1, /device:TPU:8, one launch (start us, length us, event | category | flops | bytes accessed | tf_op | source)
XLA Modules:
  0.0 676.8 jit_solution(6967788535254718402)
XLA Ops:
  7.2 0.7 all-gather.3.cloned.1.call-update
  8.0 0.7 all-gather.5.cloned.1.call-update
  8.7 0.9 fusion.208
  9.6 0.8 slice_reduce_fusion.1
  10.4 1.3 slice_bitcast_fusion.1
  11.8 33.8 %while.42 = (s32[]{:T(128)}, bf16[2,1024,128]{2,1,0:T(8,128)(2,1)S(1)}, s32[2,8,1024]{2,1,0:T(8,128)S(1)}, s32[2,1024]{1,0:T(2,128)S(1)}, bf16[2048,128]{1,0:T(8...) while((s32[]{:T(128)}, ...), condition=%wide.region_1.2_spmd, body=%wide.region_0.1_spmd.sunk | while | flops 620765184 | bytes 1167617 | solution.py:41
  11.9 16.7 %fusion.244 = bf16[2,1024,128]{2,1,0:T(8,128)(2,1)S(1)} fusion(bf16[2,1024,128]{2,1,0:T(8,128)(2,1)S(1)} %get-tuple-element.597, s32[]{:T(128)} %get-tuple-element.596, bf16[2048,128]{1,0:T(8,128)(2,1)S(1)} %get-tuple-element.614, s32[1024]{0:T(1024)S(1)} %bitcast.227, s32[1024]{0:T(1024)S(1)} %bitcast.221, s32[1024]{0:T(1024)S(1)} %bitcast.222, ...), kind=kOutput, calls=%fused_computation.41.clone.1 | convolution fusion | flops 620756992 | bytes 1089540 | tf_op jit(solution)/shard_map/while/body/eval_jaxpr/dot_general | solution.py:39
  28.8 16.7 %fusion.244 = bf16[2,1024,128]{2,1,0:T(8,128)(2,1)S(1)} fusion(bf16[2,1024,128]{2,1,0:T(8,128)(2,1)S(1)} %get-tuple-element.597, s32[]{:T(128)} %get-tuple-element.596, bf16[2048,128]{1,0:T(8,128)(2,1)S(1)} %get-tuple-element.614, s32[1024]{0:T(1024)S(1)} %bitcast.227, s32[1024]{0:T(1024)S(1)} %bitcast.221, s32[1024]{0:T(1024)S(1)} %bitcast.222, ...), kind=kOutput, calls=%fused_computation.41.clone.1 | convolution fusion | flops 620756992 | bytes 1089540 | tf_op jit(solution)/shard_map/while/body/eval_jaxpr/dot_general | solution.py:39
  45.7 33.8 %while.43 = (s32[]{:T(128)}, bf16[2,1024,128]{2,1,0:T(8,128)(2,1)S(1)}, s32[2,8,1024]{2,1,0:T(8,128)S(1)}, s32[2,1024]{1,0:T(2,128)S(1)}, bf16[2048,128]{1,0:T(8...) while((s32[]{:T(128)}, ...), condition=%wide.region_3.4_spmd, body=%wide.region_2.3_spmd.sunk | while | flops 620765184 | bytes 1167617 | solution.py:41
  45.8 16.7 %fusion.247 = bf16[2,1024,128]{2,1,0:T(8,128)(2,1)S(1)} fusion(bf16[2,1024,128]{2,1,0:T(8,128)(2,1)S(1)} %get-tuple-element.555, s32[]{:T(128)} %get-tuple-element.554, bf16[2048,128]{1,0:T(8,128)(2,1)S(1)} %get-tuple-element.572, s32[1024]{0:T(1024)S(1)} %bitcast.235, s32[1024]{0:T(1024)S(1)} %bitcast.229, s32[1024]{0:T(1024)S(1)} %bitcast.230, ...), kind=kOutput, calls=%fused_computation.100.clone.1 | convolution fusion | flops 620756992 | bytes 1089540 | tf_op jit(solution)/shard_map/while/body/eval_jaxpr/dot_general | solution.py:39
  62.7 16.7 %fusion.247 = bf16[2,1024,128]{2,1,0:T(8,128)(2,1)S(1)} fusion(bf16[2,1024,128]{2,1,0:T(8,128)(2,1)S(1)} %get-tuple-element.555, s32[]{:T(128)} %get-tuple-element.554, bf16[2048,128]{1,0:T(8,128)(2,1)S(1)} %get-tuple-element.572, s32[1024]{0:T(1024)S(1)} %bitcast.235, s32[1024]{0:T(1024)S(1)} %bitcast.229, s32[1024]{0:T(1024)S(1)} %bitcast.230, ...), kind=kOutput, calls=%fused_computation.100.clone.1 | convolution fusion | flops 620756992 | bytes 1089540 | tf_op jit(solution)/shard_map/while/body/eval_jaxpr/dot_general | solution.py:39
  79.6 9.5 %copy.44 = bf16[2048,2,128]{2,1,0:T(2,128)(2,1)} copy(bf16[2048,2,128]{2,0,1:T(8,128)(2,1)S(1)} %pad_maximum_fusion.1) | data formatting | bytes 2097152 | tf_op jit(solution)/shard_map/stack | solution.py:128
  89.1 9.8 %all-to-all-start = ((bf16[2048,2,128]{2,1,0:T(2,128)(2,1)}), bf16[2048,2,128]{2,1,0:T(2,128)(2,1)S(1)}, u32[]{:S(2)}, u32[]{:S(2)}) async-start(bf16[2048,2,128]{2,1,0:T(2,128)(2,1)} %copy.44), calls=%async_computation | async-start | bytes 2097152 | tf_op jit(solution)/shard_map/all_to_all | solution.py:137
  99.0 0.2 convolution_add_fusion.2
  99.5 0.2 convolution_add_fusion.4
  99.9 24.2 %all-to-all-done = bf16[2048,2,128]{2,1,0:T(2,128)(2,1)S(1)} async-done(((bf16[2048,2,128]{2,1,0:T(2,128)(2,1)}), bf16[2048,2,128]{2,1,0:T(2,128)(2,1)S(1)}, u32[]{:S(2)}, u32[]{:S(2)}) %all-to-all-start) | async-done | bytes 1048608 | tf_op jit(solution)/shard_map/all_to_all | solution.py:137
  124.2 1.1 copy.46
  125.3 0.5 fusion.191
  125.9 0.5 pad_maximum_fusion.2
  126.4 1.3 copy.49
  127.7 1.0 copy.50
  128.8 6.5 fusion.187
  135.3 5.4 fusion.188
  140.7 1.0 copy.51
  141.8 1.0 slice.188
  142.7 1.9 copy.52
  144.7 0.5 fusion.192
  145.2 1.4 copy.53
  146.6 6.3 all-to-all-start.1
  152.9 0.6 convert_reduce_fusion.2
  153.6 0.8 convert_reduce_fusion.1
  154.3 0.9 fusion.204
  155.2 1.1 fusion.205
  156.4 120.2 %all-reduce.9.cloned.1.call-done = (f32[512,256]{1,0:T(8,128)}, f32[256,128]{1,0:T(8,128)}) async-done(((f32[512,256]{1,0:T(8,128)}, f32[256,128]{1,0:T(8,128)}), (f32[512,256]{1,0:T(8,128)}, f32[256,128]{1,0:T(8,128)})) %all-reduce.9.cloned.1.call-update) | async-done | bytes 655376 | tf_op jit(solution)/shard_map/psum | solution.py:202
  276.9 30.7 %while.44 = (s32[]{:T(128)}, f32[2048,128]{1,0:T(8,128)}, s32[2,8,1024]{2,1,0:T(8,128)S(1)}, s32[2,1024]{1,0:T(2,128)S(1)}, bf16[2,1024,128]{2,1,0:T(8,128)(2,1)...) while((s32[]{:T(128)}, f32[2048,128]{1,0:T(8,128)}, ...), condition=%wide.region_5.6_spmd.clone, body=%wide.region_4.5_spmd.clone.sunk | while | flops 621289472 | bytes 2478347 | solution.py:56
  277.3 14.5 %fusion.250 = f32[2048,128]{1,0:T(8,128)} fusion(s32[1024]{0:T(1024)S(1)} %bitcast.211, s32[1024]{0:T(1024)S(1)} %bitcast.205, s32[1024]{0:T(1024)S(1)} %bitcast.206, s32[1024]{0:T(1024)S(1)} %bitcast.207, s32[1024]{0:T(1024)S(1)} %bitcast.208, s32[1024]{0:T(1024)S(1)} %bitcast.209, s32[1024]{0:T(1024)S(1)} %bitcast.210, s32[1024]{0:T(1024)S(1)} %bitcast.204, ...), kind=kOutput, calls=%fused_computation.166.clone.1 | convolution fusion | flops 621281280 | bytes 2400261 | tf_op jit(solution)/shard_map/while/body/eval_jaxpr/dot_general | solution.py:51
  291.9 15.7 %fusion.250 = f32[2048,128]{1,0:T(8,128)} fusion(s32[1024]{0:T(1024)S(1)} %bitcast.211, s32[1024]{0:T(1024)S(1)} %bitcast.205, s32[1024]{0:T(1024)S(1)} %bitcast.206, s32[1024]{0:T(1024)S(1)} %bitcast.207, s32[1024]{0:T(1024)S(1)} %bitcast.208, s32[1024]{0:T(1024)S(1)} %bitcast.209, s32[1024]{0:T(1024)S(1)} %bitcast.210, s32[1024]{0:T(1024)S(1)} %bitcast.204, ...), kind=kOutput, calls=%fused_computation.166.clone.1 | convolution fusion | flops 621281280 | bytes 2400261 | tf_op jit(solution)/shard_map/while/body/eval_jaxpr/dot_general | solution.py:51
  307.6 27.9 %while.45 = (s32[]{:T(128)}, f32[2048,128]{1,0:T(8,128)S(1)}, s32[2,8,1024]{2,1,0:T(8,128)S(1)}, s32[2,1024]{1,0:T(2,128)S(1)}, bf16[2,1024,128]{2,1,0:T(8,128)(...) while((s32[]{:T(128)}, f32[2048,128]{1,0:T(8,128)S(1)}, ...), condition=%wide.region_7.8_spmd.clone, body=%wide.region_6.7_spmd.clone.sunk | while | flops 621289472 | bytes 2478347 | solution.py:56
  308.0 13.7 %fusion.253 = f32[2048,128]{1,0:T(8,128)S(1)} fusion(s32[1024]{0:T(1024)S(1)} %bitcast.219, s32[1024]{0:T(1024)S(1)} %bitcast.213, s32[1024]{0:T(1024)S(1)} %bitcast.214, s32[1024]{0:T(1024)S(1)} %bitcast.215, s32[1024]{0:T(1024)S(1)} %bitcast.216, s32[1024]{0:T(1024)S(1)} %bitcast.217, s32[1024]{0:T(1024)S(1)} %bitcast.218, ...), kind=kOutput, calls=%fused_computation.235.clone.1 | convolution fusion | flops 621281280 | bytes 2400261 | tf_op jit(solution)/shard_map/while/body/eval_jaxpr/dot_general | solution.py:51
  321.9 13.7 %fusion.253 = f32[2048,128]{1,0:T(8,128)S(1)} fusion(s32[1024]{0:T(1024)S(1)} %bitcast.219, s32[1024]{0:T(1024)S(1)} %bitcast.213, s32[1024]{0:T(1024)S(1)} %bitcast.214, s32[1024]{0:T(1024)S(1)} %bitcast.215, s32[1024]{0:T(1024)S(1)} %bitcast.216, s32[1024]{0:T(1024)S(1)} %bitcast.217, s32[1024]{0:T(1024)S(1)} %bitcast.218, ...), kind=kOutput, calls=%fused_computation.235.clone.1 | convolution fusion | flops 621281280 | bytes 2400261 | tf_op jit(solution)/shard_map/while/body/eval_jaxpr/dot_general | solution.py:51
  335.6 2.9 pad_maximum_fusion
  338.5 0.3 fusion.189
  338.8 0.2 convert_reduce_fusion
  339.3 47.9 %all-reduce.2 = (f32[13,512]{1,0:T(8,128)S(1)}, f32[512]{0:T(512)S(1)}, f32[256]{0:T(256)S(1)}, f32[128]{0:T(128)S(1)}, f32[3456]{0:T(1024)S(1)}) all-reduce(f32[13,512]{1,0:T(8,128)S(1)} %convolution_bitcast_fusion, f32[512]{0:T(512)S(1)} %get-tuple-element.284, ...), channel_id=1, replica_groups=mesh['dp'=32,'table'=16] {'table'}, use_global_device_ids=true, to_apply=%region_9.10 | all-reduce | flops 11008 | bytes 88064 | tf_op jit(solution)/shard_map/psum | solution.py:202
  387.1 143.6 %all-reduce = (f32[13,512]{1,0:T(8,128)}, f32[512]{0:T(512)}, f32[256]{0:T(256)}, f32[128]{0:T(128)}, f32[3456]{0:T(1024)}) all-reduce(f32[13,512]{1,0:T(8,128)S(1)} %get-tuple-element.237, f32[512]{0:T(512)S(1)} %get-tuple-element.238, f32[256]{0:T(256)S(1)} %get-tuple-element.239, ...), channel_id=1, replica_groups=mesh['dp'=32,'table'=16] {'dp'}, use_global_device_ids=true, to_apply=%region_10.11 | all-reduce | flops 11008 | bytes 88064 | tf_op jit(solution)/shard_map/psum | solution.py:203
  530.7 135.7 %reduce-scatter.2.cloned.1.call-done = f32[2,64,128]{2,1,0:T(8,128)} async-done(((f32[2,2048,128]{2,1,0:T(8,128)}), f32[2,64,128]{2,1,0:T(8,128)}) %reduce-scatter.2.cloned.1.call-update) | async-done | bytes 65552 | tf_op jit(solution)/shard_map/reduce_scatter | solution.py:191
  666.4 1.9 copy.87
  668.3 1.6 copy.88
  (88 shorter events, 2.8 us)
Async XLA Ops:
  7.2 92.0 %copy-start = (bf16[512,256]{1,0:T(8,128)(2,1)S(1)}, bf16[512,256]{1,0:T(8,128)(2,1)}, u32[]{:S(2)}) copy-start(bf16[512,256]{1,0:T(8,128)(2,1)} %param.30) | copy-start | bytes 786436
  7.2 121.6 %all-gather.3.cloned.1.call-start = ((), (), s32[]{:S(2)}) async-start(), calls=%async_computation.3 | async-start | bytes 3760128 | tf_op jit(solution)/shard_map/all_gather | solution.py:156
  7.9 120.9 %all-gather.5.cloned.1.call-start = ((), (), s32[]{:S(2)}) async-start(), calls=%async_computation.4 | async-start | bytes 3760128 | tf_op jit(solution)/shard_map/all_gather | solution.py:157
  79.5 19.5 %copy-start.7 = (bf16[13,512]{1,0:T(8,128)(2,1)S(1)}, bf16[13,512]{1,0:T(8,128)(2,1)}, u32[]{:S(2)}) copy-start(bf16[13,512]{1,0:T(8,128)(2,1)} %param.28) | copy-start | bytes 39940
  79.5 19.5 %copy-start.8 = (bf16[128,13]{0,1:T(8,128)(2,1)S(1)}, bf16[128,13]{0,1:T(8,128)(2,1)}, u32[]{:S(2)}) copy-start(bf16[128,13]{0,1:T(8,128)(2,1)} %param.23) | copy-start | bytes 9988
  79.5 19.5 %copy-start.10 = (f32[512]{0:T(512)S(1)}, f32[512]{0:T(512)}, u32[]{:S(2)}) copy-start(f32[512]{0:T(512)} %param.29) | copy-start | bytes 6148
  79.5 19.7 %copy-start.17 = (f32[256]{0:T(256)S(1)}, f32[256]{0:T(256)}, u32[]{:S(2)}) copy-start(f32[256]{0:T(256)} %param.31) | copy-start | bytes 3076
  79.5 19.9 %copy-start.15 = (bf16[256,128]{1,0:T(8,128)(2,1)S(1)}, bf16[256,128]{1,0:T(8,128)(2,1)}, u32[]{:S(2)}) copy-start(bf16[256,128]{1,0:T(8,128)(2,1)} %param.32) | copy-start | bytes 196612
  79.5 19.9 %copy-start.18 = (f32[128]{0:T(128)S(1)}, f32[128]{0:T(128)}, u32[]{:S(2)}) copy-start(f32[128]{0:T(128)} %param.33) | copy-start | bytes 1540
  89.1 34.9 %all-to-all-start = ((bf16[2048,2,128]{2,1,0:T(2,128)(2,1)}), bf16[2048,2,128]{2,1,0:T(2,128)(2,1)S(1)}, u32[]{:S(2)}, u32[]{:S(2)}) async-start(bf16[2048,2,128]{2,1,0:T(2,128)(2,1)} %copy.44), calls=%async_computation | async-start | bytes 2097152 | tf_op jit(solution)/shard_map/all_to_all | solution.py:137
  99.0 26.3 %copy-start.11 = (s32[32]{0:T(128)S(1)}, s32[32]{0:T(128)}, u32[]{:S(2)}) copy-start(s32[32]{0:T(128)} %param.26) | copy-start | bytes 388
  99.2 56.0 %copy-start.5 = (f32[128,512]{1,0:T(8,128)}, f32[128,512]{1,0:T(8,128)S(1)}, u32[]{:S(2)}) copy-start(f32[128,512]{1,0:T(8,128)S(1)} %convolution_add_fusion.2) | copy-start | bytes 786436
  99.5 26.4 %copy-start.19 = (f32[128,256]{1,0:T(8,128)}, f32[128,256]{1,0:T(8,128)S(1)}, u32[]{:S(2)}) copy-start(f32[128,256]{1,0:T(8,128)S(1)} %convolution_add_fusion.3) | copy-start | bytes 393220
  125.3 3.5 copy-start.3
  128.7 6.6 copy-start.1
  140.7 3.9 copy-start.12
  144.7 8.9 %copy-start.16 = (bf16[256,128]{1,0:T(8,128)(2,1)S(1)}, bf16[256,128]{1,0:T(8,128)(2,1)}, u32[]{:S(2)}) copy-start(bf16[256,128]{1,0:T(8,128)(2,1)} %param.32) | copy-start | bytes 196612
  144.7 8.9 %copy-start.20 = (f32[128,256]{1,0:T(8,128)S(1)}, f32[128,256]{1,0:T(8,128)}, u32[]{:S(2)}) copy-start(f32[128,256]{1,0:T(8,128)} %copy-done.19) | copy-start | bytes 393220
  146.6 130.2 %all-to-all-start.1 = ((bf16[128,32,128]{2,0,1:T(8,128)(2,1)}), bf16[128,32,128]{2,0,1:T(8,128)(2,1)S(1)}, u32[]{:S(2)}, u32[]{:S(2)}) async-start(bf16[128,32,128]{2,0,1:T(8,128)(2,1)} %copy.53), calls=%async_computation.1 | async-start | bytes 2097152 | tf_op jit(solution)/shard_map/all_to_all | solution.py:177
  152.9 123.8 %all-reduce.9.cloned.1.call-start = ((), (), s32[]{:S(2)}) async-start(), calls=%async_computation.7 | async-start | bytes 1310720 | tf_op jit(solution)/shard_map/psum | solution.py:202
  154.3 2.1 copy-start.21
  156.3 374.4 %all-reduce.7.cloned.1.call-start = ((), (), s32[]{:S(2)}) async-start(), calls=%async_computation.6 | async-start | bytes 1310720 | tf_op jit(solution)/shard_map/psum | solution.py:203
  276.7 389.8 %reduce-scatter.2.cloned.1.call-start = ((), (), s32[]{:S(2)}) async-start(), calls=%async_computation.5 | async-start | bytes 2162688 | tf_op jit(solution)/shard_map/reduce_scatter | solution.py:191
  335.5 2.9 copy-start.2
  335.6 2.9 copy-start.4
  335.6 3.2 copy-start.6
  335.6 3.2 copy-start.22
  338.4 0.7 copy-start.9
  338.4 0.8 copy-start.13
  338.4 0.8 copy-start.14
Sparse Core Ops, SparseCore 0:
  10.1 48.4 all-gather.2
  60.7 47.3 all-gather.4
  156.7 119.8 all-reduce.8
  280.3 162.2 all-reduce.6
  447.4 218.9 reduce-scatter.1
